TPU v7x, 32 devices: a whole 2x2x4 slice. The times are simulated.
32 devices in a mesh: slab: 8 (over z, x), leaf: 4 (over y, core).
Axes of the slice: x: 2, y: 2, z: 4, core: 2. Of those that a mesh axis runs over, the one named last changes fastest.
Arguments:
- particles: float32 [3, 32, 16, 256], P(None, 'slab', 'leaf'), may hold values from -1.05 to 1.05, as said below
- near_mask: int32 [16, 32, 16], P(None, 'slab', 'leaf'), may hold values from 0 to 1, as said below
Outputs:
- velocity: float32 [2, 32, 16, 256], P(None, 'slab', 'leaf')
Inputs may be any that keep to these rules, and one draw needn't show every extreme that they name: `particles`: entries 0 and 1 of the first dimension are offsets; entry 2 is the circulation. near_mask[o, i, j] = near_mask[15 - o, i + dx, j + dy], where (dx, dy) is step o of the 16 steps with max(|dx|, |dy|) = 2 in row-major order over dx, then dy; it is 0 where leaf (i + dx, j + dy) lies outside the grid.
All inputs are finite; a program needn't handle non-finite values.
Results may differ from a plain program's by a relative error of at most 0.0003.
Values sent between devices are 32-bit elements; how exact they have to be, the bound alone decides.
A program may use at most 64 MiB of HBM per device.

v0:
```python
import math

import jax
import jax.numpy as jnp
import numpy as np
from jax import lax
from jax.sharding import PartitionSpec as P

ORDER = 10


DELTA_SQUARED = 0.0025
TWO_PI = 2.0 * math.pi
inner_steps = [(a, b) for a in range(-1, 2) for b in range(-1, 2)]
cycle_steps = [(a, b) for a in range(-2, 3) for b in range(-2, 3) if max(abs(a), abs(b)) == 2]


def with_halo(shard, sides, width):
    for axis, dim in sides:
        size, length = (lax.axis_size(axis), shard.shape[dim])
        up = [(i, (i + 1) % size) for i in range(size - 1)]
        down = [(j, i) for i, j in up]
        last = lax.slice_in_dim(shard, length - width, length, axis=dim)
        first = lax.slice_in_dim(shard, 0, width, axis=dim)
        before = lax.ppermute(last, axis, up)
        after = lax.ppermute(first, axis, down)
        shard = jnp.concatenate([before, shard, after], axis=dim)
    return shard


def complex_powers(base_real, base_imaginary, count):
    power_real = [jnp.ones_like(base_real)]
    power_imaginary = [jnp.zeros_like(base_imaginary)]
    for repeat in range(1, count):
        last_real = power_real[-1]
        last_imaginary = power_imaginary[-1]
        power_real.append(last_real * base_real - last_imaginary * base_imaginary)
        power_imaginary.append(last_real * base_imaginary + last_imaginary * base_real)
    return (jnp.stack(power_real, -1), jnp.stack(power_imaginary, -1))


def translation(shift_real, shift_imaginary):
    hankel = np.arange(ORDER)[:, None] + np.arange(ORDER)[None, :] + 1
    weights = np.array(
        [[math.comb(i + k, k) * (-1.0) ** (k + 1) for k in range(ORDER)] for i in range(ORDER)],
        dtype=np.float32,
    )
    denominator = shift_real * shift_real + shift_imaginary * shift_imaginary
    inverse_real = shift_real / denominator
    inverse_imaginary = -shift_imaginary / denominator
    power_real, power_imaginary = complex_powers(inverse_real, inverse_imaginary, 2 * ORDER)
    return (power_real[..., hankel] * weights, power_imaginary[..., hankel] * weights)


def upward_shift(everything, centred):
    block_side = centred.shape[0]
    shift_real = jnp.broadcast_to(centred[:, None], (block_side, block_side))
    shift_imaginary = jnp.broadcast_to(centred[None, :], (block_side, block_side))
    power_real, power_imaginary = complex_powers(shift_real, shift_imaginary, ORDER)
    lower = np.arange(ORDER)
    gaps = np.maximum(lower[:, None] - lower[None, :], 0)
    binomial = np.array(
        [[math.comb(k, m) if m <= k else 0 for m in range(ORDER)] for k in range(ORDER)],
        dtype=np.float32,
    )
    shift_matrix_real = power_real[..., gaps] * binomial
    shift_matrix_imaginary = power_imaginary[..., gaps] * binomial
    source_real = everything[:, 0]
    source_imaginary = everything[:, 1]
    highest = lax.Precision.HIGHEST
    block_real = jnp.einsum(
        "nijm,ijkm->nk", source_real, shift_matrix_real, precision=highest
    ) - jnp.einsum("nijm,ijkm->nk", source_imaginary, shift_matrix_imaginary, precision=highest)
    block_imaginary = jnp.einsum(
        "nijm,ijkm->nk", source_real, shift_matrix_imaginary, precision=highest
    ) + jnp.einsum("nijm,ijkm->nk", source_imaginary, shift_matrix_real, precision=highest)
    return jnp.stack([block_real, block_imaginary], axis=1)


def body(particles, near_mask):
    block_side = particles.shape[1]
    highest = lax.Precision.HIGHEST
    slab_index = lax.axis_index("slab")
    leaf_index = lax.axis_index("leaf")
    slab_count = lax.axis_size("slab")
    leaf_count = lax.axis_size("leaf")
    device_count = slab_count * leaf_count
    offset_x, offset_y, strength = (particles[0], particles[1], particles[2])
    power_real, power_imaginary = complex_powers(offset_x, offset_y, ORDER)
    leaf_multipole = jnp.stack(
        [
            jnp.sum(strength[..., None] * power_real, axis=2),
            jnp.sum(strength[..., None] * power_imaginary, axis=2),
        ]
    )
    centred = jnp.arange(block_side, dtype=jnp.float32) - (block_side - 1) / 2.0
    everything = lax.all_gather(leaf_multipole[None], ("slab", "leaf"), axis=0, tiled=True)
    grid = everything.reshape(slab_count, leaf_count, 2, block_side, block_side, ORDER).transpose(
        2, 0, 3, 1, 4, 5
    )
    grid = grid.reshape(2, slab_count * block_side, leaf_count * block_side, ORDER)
    padded_grid = jnp.pad(
        grid, ((0, 0), (block_side, block_side), (block_side, block_side), (0, 0))
    )
    window = lax.dynamic_slice(
        padded_grid,
        (jnp.int32(0), slab_index * block_side, leaf_index * block_side, jnp.int32(0)),
        (2, 3 * block_side, 3 * block_side, ORDER),
    )
    blocks = upward_shift(everything, centred)
    near = with_halo(particles, (("slab", 1), ("leaf", 2)), 2)
    mask_float = near_mask.astype(jnp.float32)

    def direct_row(row):
        target_x = offset_x[row]
        target_y = offset_y[row]
        row_real = jnp.zeros(target_x.shape, jnp.float32)
        row_imaginary = jnp.zeros(target_x.shape, jnp.float32)
        for number, (step_x, step_y) in enumerate(inner_steps + cycle_steps):
            source_row = lax.dynamic_index_in_dim(near, 2 + step_x + row, 1, keepdims=False)
            source = source_row[:, 2 + step_y : 2 + step_y + block_side, :]
            if number < 9:
                circulation = source[2]
            else:
                mask_row = lax.dynamic_index_in_dim(mask_float[number - 9], row, 0, keepdims=False)
                circulation = source[2] * mask_row[:, None]
            delta_x = target_x[:, :, None] - (step_x + source[0][:, None, :])
            delta_y = target_y[:, :, None] - (step_y + source[1][:, None, :])
            factor = circulation[:, None, :] / (
                delta_x * delta_x + delta_y * delta_y + DELTA_SQUARED
            )
            row_real = row_real + jnp.sum(factor * delta_x, -1)
            row_imaginary = row_imaginary - jnp.sum(factor * delta_y, -1)
        return (row_real, row_imaginary)

    sum_real, sum_imaginary = lax.map(direct_row, jnp.arange(block_side, dtype=jnp.int32))
    margin = block_side - 1
    outer = 2 * block_side - 1
    padded_window = jnp.pad(window, ((0, 0), (margin, margin), (margin, margin), (0, 0)))
    far_list = [
        (a, b)
        for a in range(-outer, outer + 1)
        for b in range(-outer, outer + 1)
        if max(abs(a), abs(b)) >= 3
    ]
    step_table = np.array(cycle_steps + far_list, dtype=np.int32)
    group_count = 2 * (block_side - 1)
    group_size = step_table.shape[0] // group_count
    weights = jnp.concatenate(
        [1.0 - mask_float, jnp.ones((len(far_list), block_side, block_side), jnp.float32)]
    )
    weights = weights.reshape(group_count, group_size, block_side, block_side)
    grouped_table = jnp.asarray(step_table.reshape(group_count, group_size, 2))
    place = jnp.arange(block_side, dtype=jnp.int32)

    def leaf_group(totals, pieces):
        table, weight = pieces
        rows = outer + table[:, 0][:, None] + place[None, :]
        columns = outer + table[:, 1][:, None] + place[None, :]
        sources = (
            padded_window[:, rows[:, :, None], columns[:, None, :], :] * weight[None, :, :, :, None]
        )
        matrix_real, matrix_imaginary = translation(
            table[:, 0].astype(jnp.float32), table[:, 1].astype(jnp.float32)
        )
        part_real = jnp.einsum(
            "sijk,slk->ijl", sources[0], matrix_real, precision=highest
        ) - jnp.einsum("sijk,slk->ijl", sources[1], matrix_imaginary, precision=highest)
        part_imaginary = jnp.einsum(
            "sijk,slk->ijl", sources[0], matrix_imaginary, precision=highest
        ) + jnp.einsum("sijk,slk->ijl", sources[1], matrix_real, precision=highest)
        return ((totals[0] + part_real, totals[1] + part_imaginary), None)

    zero_local = jnp.zeros((block_side, block_side, ORDER), jnp.float32)
    (local_real, local_imaginary), unused = lax.scan(
        leaf_group, (zero_local, zero_local), (grouped_table, weights)
    )
    device_number = np.arange(device_count)
    block_x = jnp.asarray(device_number // leaf_count, jnp.int32)
    block_y = jnp.asarray(device_number % leaf_count, jnp.int32)
    global_x = (slab_index * block_side + jnp.arange(block_side, dtype=jnp.int32)).astype(
        jnp.float32
    )
    global_y = (leaf_index * block_side + jnp.arange(block_side, dtype=jnp.int32)).astype(
        jnp.float32
    )
    remote = jnp.maximum(jnp.abs(block_x - slab_index), jnp.abs(block_y - leaf_index)) >= 2
    centre_x = (block_x * block_side).astype(jnp.float32) + (block_side - 1) / 2.0
    centre_y = (block_y * block_side).astype(jnp.float32) + (block_side - 1) / 2.0
    far_blocks = blocks * remote.astype(jnp.float32)[:, None, None]
    block_groups = device_count // 8

    def block_group(totals, pieces):
        group_x, group_y, group_remote, group_blocks = pieces
        grid_shape = (8, block_side, block_side)
        shift_real = jnp.broadcast_to(group_x[:, None, None] - global_x[None, :, None], grid_shape)
        shift_imaginary = jnp.broadcast_to(
            group_y[:, None, None] - global_y[None, None, :], grid_shape
        )
        shift_real = jnp.where(group_remote[:, None, None], shift_real, 1.0)
        shift_imaginary = jnp.where(group_remote[:, None, None], shift_imaginary, 1.0)
        matrix_real, matrix_imaginary = translation(shift_real, shift_imaginary)
        part_real = jnp.einsum(
            "nijlk,nk->ijl", matrix_real, group_blocks[:, 0], precision=highest
        ) - jnp.einsum("nijlk,nk->ijl", matrix_imaginary, group_blocks[:, 1], precision=highest)
        part_imaginary = jnp.einsum(
            "nijlk,nk->ijl", matrix_imaginary, group_blocks[:, 0], precision=highest
        ) + jnp.einsum("nijlk,nk->ijl", matrix_real, group_blocks[:, 1], precision=highest)
        return ((totals[0] + part_real, totals[1] + part_imaginary), None)

    block_pieces = (
        centre_x.reshape(block_groups, 8),
        centre_y.reshape(block_groups, 8),
        remote.reshape(block_groups, 8),
        far_blocks.reshape(block_groups, 8, 2, ORDER),
    )
    (local_real, local_imaginary), unused = lax.scan(
        block_group, (local_real, local_imaginary), block_pieces
    )
    sum_real = sum_real + jnp.sum(
        local_real[:, :, None, :] * power_real - local_imaginary[:, :, None, :] * power_imaginary,
        -1,
    )
    sum_imaginary = sum_imaginary + jnp.sum(
        local_real[:, :, None, :] * power_imaginary + local_imaginary[:, :, None, :] * power_real,
        -1,
    )
    return jnp.stack([sum_imaginary, sum_real]) / TWO_PI


def solution(mesh):
    return jax.shard_map(
        body,
        mesh=mesh,
        in_specs=(P(None, "slab", "leaf", None), P(None, "slab", "leaf")),
        out_specs=P(None, "slab", "leaf", None),
        check_vma=False,
    )
```

profile of v0, /device:TPU:0, one launch (start us, length us, event | category | flops | bytes accessed | tf_op | source)
XLA Modules:
  0.0 320.3 jit_solution(4241065399967173239)
XLA Ops:
  0.8 4.8 %collective-permute-start = (f32[3,2,4,256]{3,2,0,1:T(4,128)S(1)}, f32[3,2,4,256]{3,2,0,1:T(4,128)S(1)}, u32[]{:S(2)}, u32[]{:S(2)}) collective-permute-start(f32[3,2,4,256]{3,2,0,1:T(4,128)S(1)} %copy.289), channel_id=1, source_target_pairs={{0,4},{4,8},{8,12},{12,16},{16,20},{20,24},{24,28},{1,5},{5,9},{9,... | collective-permute-start | bytes 73736 | tf_op jit(solution)/shard_map/ppermute | solution.py:25
  20.3 44.4 %all-gather = f32[64,4,4,10]{3,2,1,0:T(4,128)S(1)} all-gather(f32[2,4,4,10]{3,2,1,0:T(4,128)S(1)} %pad_maximum_fusion.1), channel_id=2, replica_groups=mesh['slab'=8,'leaf'=4] {'slab','leaf'}, dimensions={0}, use_global_device_ids=true | all-gather | bytes 42240 | tf_op jit(solution)/shard_map/all_gather | solution.py:97
  65.5 57.2 %while.46 = (s32[]{:T(128)}, f32[4,4,10]{2,1,0:T(4,128)S(1)}, f32[4,4,10]{2,1,0:T(4,128)S(1)}, f32[2,18,18,10]{3,0,2,1:T(2,128)S(1)}, f32[6,36,4,4]{1,3,2,0:T(4,...) while((s32[]{:T(128)}, f32[4,4,10]{2,1,0:T(4,128)S(1)}, ...), condition=%wide.region_55.56_spmd.clone.clone.clone, body=%wide.region_54.55_spmd.sunk.clone.clone.clone.sunk | while | flops 2792347 | bytes 1186424 | solution.py:175
  68.2 4.9 %gather_fusion.4 = f32[576,2,10]{2,1,0:T(2,128)S(1)} fusion(f32[2,18,18,10]{3,0,2,1:T(2,128)S(1)} %get-tuple-element.1451, s32[576]{0:T(1024)S(1)} %reshape.10059), kind=kCustom, calls=%fused_computation.clone.clone.clone.1 | custom fusion | bytes 96768 | tf_op jit(solution)/shard_map/while/body/eval_jaxpr/gather | solution.py:161
  77.7 4.9 %gather_fusion.4 = f32[576,2,10]{2,1,0:T(2,128)S(1)} fusion(f32[2,18,18,10]{3,0,2,1:T(2,128)S(1)} %get-tuple-element.1451, s32[576]{0:T(1024)S(1)} %reshape.10059), kind=kCustom, calls=%fused_computation.clone.clone.clone.1 | custom fusion | bytes 96768 | tf_op jit(solution)/shard_map/while/body/eval_jaxpr/gather | solution.py:161
  87.3 4.9 %gather_fusion.4 = f32[576,2,10]{2,1,0:T(2,128)S(1)} fusion(f32[2,18,18,10]{3,0,2,1:T(2,128)S(1)} %get-tuple-element.1451, s32[576]{0:T(1024)S(1)} %reshape.10059), kind=kCustom, calls=%fused_computation.clone.clone.clone.1 | custom fusion | bytes 96768 | tf_op jit(solution)/shard_map/while/body/eval_jaxpr/gather | solution.py:161
  96.8 4.9 %gather_fusion.4 = f32[576,2,10]{2,1,0:T(2,128)S(1)} fusion(f32[2,18,18,10]{3,0,2,1:T(2,128)S(1)} %get-tuple-element.1451, s32[576]{0:T(1024)S(1)} %reshape.10059), kind=kCustom, calls=%fused_computation.clone.clone.clone.1 | custom fusion | bytes 96768 | tf_op jit(solution)/shard_map/while/body/eval_jaxpr/gather | solution.py:161
  106.3 4.9 %gather_fusion.4 = f32[576,2,10]{2,1,0:T(2,128)S(1)} fusion(f32[2,18,18,10]{3,0,2,1:T(2,128)S(1)} %get-tuple-element.1451, s32[576]{0:T(1024)S(1)} %reshape.10059), kind=kCustom, calls=%fused_computation.clone.clone.clone.1 | custom fusion | bytes 96768 | tf_op jit(solution)/shard_map/while/body/eval_jaxpr/gather | solution.py:161
  115.9 4.9 %gather_fusion.4 = f32[576,2,10]{2,1,0:T(2,128)S(1)} fusion(f32[2,18,18,10]{3,0,2,1:T(2,128)S(1)} %get-tuple-element.1451, s32[576]{0:T(1024)S(1)} %reshape.10059), kind=kCustom, calls=%fused_computation.clone.clone.clone.1 | custom fusion | bytes 96768 | tf_op jit(solution)/shard_map/while/body/eval_jaxpr/gather | solution.py:161
  125.1 93.8 %while.45 = (s32[]{:T(128)}, f32[4,4,10]{2,1,0:T(4,128)S(1)}, f32[4,4,10]{2,1,0:T(4,128)S(1)}, pred[4,8]{1,0:T(4,128)(4,1)S(1)}, f32[4,8]{1,0:T(4,128)}, /*index...) while((s32[]{:T(128)}, f32[4,4,10]{2,1,0:T(4,128)S(1)}, ...), condition=%wide.region_57.58_spmd.clone.clone.clone, body=%wide.region_56.57_spmd.sunk.clone.clone.clone.sunk | while | flops 970834 | bytes 1127061 | solution.py:217
  131.3 3.8 %fusion.379 = f32[1,4,4,10,1]{3,0,4,2,1:T(1,128)S(1)} fusion(f32[8,10,1,1,1]{1,2,0,4,3:T(1,128)S(1)} %bitcast.1115, f32[10,10,8,4,4]{1,0,2,4,3:T(8,128)S(1)} %copy.299, f32[10,10]{1,0:T(8,128)S(1)} %get-tuple-element.1495), kind=kOutput, calls=%fused_computation.432.clone.1 | convolution fusion | flops 166400 | bytes 52560 | tf_op jit(solution)/shard_map/while/body/eval_jaxpr/nijlk,nk->ijl/dot_general | solution.py:203
  135.1 3.8 %fusion.378 = f32[1,4,4,10,1]{3,0,4,2,1:T(1,128)S(1)} fusion(f32[8,10,1,1,1]{1,2,0,4,3:T(1,128)S(1)} %bitcast.1117, f32[10,10,8,4,4]{1,0,2,4,3:T(8,128)S(1)} %copy.299, f32[10,10]{1,0:T(8,128)S(1)} %get-tuple-element.1495), kind=kOutput, calls=%fused_computation.430.clone.1 | convolution fusion | flops 166400 | bytes 52560 | tf_op jit(solution)/shard_map/while/body/eval_jaxpr/nijlk,nk->ijl/dot_general | solution.py:208
  141.1 3.8 %fusion.380 = f32[1,4,4,10,1]{3,0,4,2,1:T(1,128)S(1)} fusion(f32[8,10,1,1,1]{1,2,0,4,3:T(1,128)S(1)} %bitcast.1118, f32[10,10,8,4,4]{1,0,2,4,3:T(8,128)S(1)} %copy.298, f32[10,10]{1,0:T(8,128)S(1)} %get-tuple-element.1495), kind=kOutput, calls=%fused_computation.428.clone.1 | convolution fusion | flops 166400 | bytes 52560 | tf_op jit(solution)/shard_map/while/body/eval_jaxpr/nijlk,nk->ijl/dot_general | solution.py:205
  144.9 3.8 %fusion.377 = f32[1,4,4,10,1]{3,0,4,2,1:T(1,128)S(1)} fusion(f32[8,10,1,1,1]{1,2,0,4,3:T(1,128)S(1)} %bitcast.1116, f32[10,10,8,4,4]{1,0,2,4,3:T(8,128)S(1)} %copy.298, f32[10,10]{1,0:T(8,128)S(1)} %get-tuple-element.1495), kind=kOutput, calls=%fused_computation.426.clone.1 | convolution fusion | flops 166400 | bytes 52560 | tf_op jit(solution)/shard_map/while/body/eval_jaxpr/nijlk,nk->ijl/dot_general | solution.py:206
  154.7 3.8 %fusion.379 = f32[1,4,4,10,1]{3,0,4,2,1:T(1,128)S(1)} fusion(f32[8,10,1,1,1]{1,2,0,4,3:T(1,128)S(1)} %bitcast.1115, f32[10,10,8,4,4]{1,0,2,4,3:T(8,128)S(1)} %copy.299, f32[10,10]{1,0:T(8,128)S(1)} %get-tuple-element.1495), kind=kOutput, calls=%fused_computation.432.clone.1 | convolution fusion | flops 166400 | bytes 52560 | tf_op jit(solution)/shard_map/while/body/eval_jaxpr/nijlk,nk->ijl/dot_general | solution.py:203
  158.5 3.8 %fusion.378 = f32[1,4,4,10,1]{3,0,4,2,1:T(1,128)S(1)} fusion(f32[8,10,1,1,1]{1,2,0,4,3:T(1,128)S(1)} %bitcast.1117, f32[10,10,8,4,4]{1,0,2,4,3:T(8,128)S(1)} %copy.299, f32[10,10]{1,0:T(8,128)S(1)} %get-tuple-element.1495), kind=kOutput, calls=%fused_computation.430.clone.1 | convolution fusion | flops 166400 | bytes 52560 | tf_op jit(solution)/shard_map/while/body/eval_jaxpr/nijlk,nk->ijl/dot_general | solution.py:208
  164.5 3.8 %fusion.380 = f32[1,4,4,10,1]{3,0,4,2,1:T(1,128)S(1)} fusion(f32[8,10,1,1,1]{1,2,0,4,3:T(1,128)S(1)} %bitcast.1118, f32[10,10,8,4,4]{1,0,2,4,3:T(8,128)S(1)} %copy.298, f32[10,10]{1,0:T(8,128)S(1)} %get-tuple-element.1495), kind=kOutput, calls=%fused_computation.428.clone.1 | convolution fusion | flops 166400 | bytes 52560 | tf_op jit(solution)/shard_map/while/body/eval_jaxpr/nijlk,nk->ijl/dot_general | solution.py:205
  168.3 3.8 %fusion.377 = f32[1,4,4,10,1]{3,0,4,2,1:T(1,128)S(1)} fusion(f32[8,10,1,1,1]{1,2,0,4,3:T(1,128)S(1)} %bitcast.1116, f32[10,10,8,4,4]{1,0,2,4,3:T(8,128)S(1)} %copy.298, f32[10,10]{1,0:T(8,128)S(1)} %get-tuple-element.1495), kind=kOutput, calls=%fused_computation.426.clone.1 | convolution fusion | flops 166400 | bytes 52560 | tf_op jit(solution)/shard_map/while/body/eval_jaxpr/nijlk,nk->ijl/dot_general | solution.py:206
  178.1 3.8 %fusion.379 = f32[1,4,4,10,1]{3,0,4,2,1:T(1,128)S(1)} fusion(f32[8,10,1,1,1]{1,2,0,4,3:T(1,128)S(1)} %bitcast.1115, f32[10,10,8,4,4]{1,0,2,4,3:T(8,128)S(1)} %copy.299, f32[10,10]{1,0:T(8,128)S(1)} %get-tuple-element.1495), kind=kOutput, calls=%fused_computation.432.clone.1 | convolution fusion | flops 166400 | bytes 52560 | tf_op jit(solution)/shard_map/while/body/eval_jaxpr/nijlk,nk->ijl/dot_general | solution.py:203
  181.8 3.8 %fusion.378 = f32[1,4,4,10,1]{3,0,4,2,1:T(1,128)S(1)} fusion(f32[8,10,1,1,1]{1,2,0,4,3:T(1,128)S(1)} %bitcast.1117, f32[10,10,8,4,4]{1,0,2,4,3:T(8,128)S(1)} %copy.299, f32[10,10]{1,0:T(8,128)S(1)} %get-tuple-element.1495), kind=kOutput, calls=%fused_computation.430.clone.1 | convolution fusion | flops 166400 | bytes 52560 | tf_op jit(solution)/shard_map/while/body/eval_jaxpr/nijlk,nk->ijl/dot_general | solution.py:208
  191.6 3.8 %fusion.377 = f32[1,4,4,10,1]{3,0,4,2,1:T(1,128)S(1)} fusion(f32[8,10,1,1,1]{1,2,0,4,3:T(1,128)S(1)} %bitcast.1116, f32[10,10,8,4,4]{1,0,2,4,3:T(8,128)S(1)} %copy.298, f32[10,10]{1,0:T(8,128)S(1)} %get-tuple-element.1495), kind=kOutput, calls=%fused_computation.426.clone.1 | convolution fusion | flops 166400 | bytes 52560 | tf_op jit(solution)/shard_map/while/body/eval_jaxpr/nijlk,nk->ijl/dot_general | solution.py:206
  205.2 3.8 %fusion.378 = f32[1,4,4,10,1]{3,0,4,2,1:T(1,128)S(1)} fusion(f32[8,10,1,1,1]{1,2,0,4,3:T(1,128)S(1)} %bitcast.1117, f32[10,10,8,4,4]{1,0,2,4,3:T(8,128)S(1)} %copy.299, f32[10,10]{1,0:T(8,128)S(1)} %get-tuple-element.1495), kind=kOutput, calls=%fused_computation.430.clone.1 | convolution fusion | flops 166400 | bytes 52560 | tf_op jit(solution)/shard_map/while/body/eval_jaxpr/nijlk,nk->ijl/dot_general | solution.py:208
  215.0 3.8 %fusion.377 = f32[1,4,4,10,1]{3,0,4,2,1:T(1,128)S(1)} fusion(f32[8,10,1,1,1]{1,2,0,4,3:T(1,128)S(1)} %bitcast.1116, f32[10,10,8,4,4]{1,0,2,4,3:T(8,128)S(1)} %copy.298, f32[10,10]{1,0:T(8,128)S(1)} %get-tuple-element.1495), kind=kOutput, calls=%fused_computation.426.clone.1 | convolution fusion | flops 166400 | bytes 52560 | tf_op jit(solution)/shard_map/while/body/eval_jaxpr/nijlk,nk->ijl/dot_general | solution.py:206
  224.8 94.9 %while.44 = (s32[]{:T(128)}, f32[4,4,256]{2,1,0:T(4,128)S(1)}, f32[4,4,256]{2,1,0:T(4,128)S(1)}, s32[4]{0:T(128)S(1)}, f32[3,8,8,256]{3,2,0,1:T(8,128)S(1)}, /*i...) while((s32[]{:T(128)}, f32[4,4,256]{2,1,0:T(4,128)S(1)}, ...), condition=%wide.region_51.52_spmd, body=%wide.region_0.51_spmd.sunk | while | flops 72145936 | bytes 1645816 | solution.py:136
  (590 shorter events, 157.3 us)
Async XLA Ops:
  0.0 16.8 %copy-start = (f32[3,4,4,256]{3,2,1,0:T(4,128)S(1)}, f32[3,4,4,256]{3,2,1,0:T(4,128)}, u32[]{:S(2)}) copy-start(f32[3,4,4,256]{3,2,1,0:T(4,128)} %param.23) | copy-start | bytes 147460
  0.8 218.4 %collective-permute-start = (f32[3,2,4,256]{3,2,0,1:T(4,128)S(1)}, f32[3,2,4,256]{3,2,0,1:T(4,128)S(1)}, u32[]{:S(2)}, u32[]{:S(2)}) collective-permute-start(f32[3,2,4,256]{3,2,0,1:T(4,128)S(1)} %copy.289), channel_id=1, source_target_pairs={{0,4},{4,8},{8,12},{12,16},{16,20},{20,24},{24,28},{1,5},{5,9},{9,... | collective-permute-start | bytes 73736 | tf_op jit(solution)/shard_map/ppermute | solution.py:25
  5.7 213.6 %collective-permute-start.1 = (f32[3,2,4,256]{3,2,0,1:T(4,128)S(1)}, f32[3,2,4,256]{3,2,0,1:T(4,128)S(1)}, u32[]{:S(2)}, u32[]{:S(2)}) collective-permute-start(f32[3,2,4,256]{3,2,0,1:T(4,128)S(1)} %copy.290), channel_id=1, source_target_pairs={{4,0},{8,4},{12,8},{16,12},{20,16},{24,20},{28,24},{5,1},{9,5},{13... | collective-permute-start | bytes 73736 | tf_op jit(solution)/shard_map/ppermute | solution.py:26
  64.8 0.7 copy-start.1
  64.8 0.7 copy-start.3
  122.7 0.7 copy-start.2
  219.3 3.8 %collective-permute-start.2 = (f32[3,8,2,256]{3,2,0,1:T(2,128)S(1)}, f32[3,8,2,256]{3,2,0,1:T(2,128)S(1)}, u32[]{:S(2)}, u32[]{:S(2)}) collective-permute-start(f32[3,8,2,256]{3,2,0,1:T(2,128)S(1)} %get-tuple-element.795), channel_id=1, source_target_pairs={{0,1},{1,2},{2,3},{4,5},{5,6},{6,7},{8,9},{9,10},{10,11},{12,13},{... | collective-permute-start | bytes 147464 | tf_op jit(solution)/shard_map/ppermute | solution.py:25
  221.6 3.1 collective-permute-start.3
where the time goes:
time: 324 us; the launch traced here: 320 us
  local copies, waits for them, and re-layouts  80.3 us (25%)
  other arithmetic  78.6 us (24%)
  matrix products  70.1 us (22%)
  blocking collectives  44.4 us (14%)
  loops' own time  35.3 us (11%)
  starting transfers between devices  9.67 us (3%)
    reduce_sum x20, other arithmetic, direct_row(): row_imaginary = row_imaginary - jnp.sum(factor * delta_y, -1)  55.9 us
    all_gather x1, blocking collectives, body(): lax.all_gather(leaf_multipole[None], ('slab', 'leaf'), axis=0, tiled=True)  44.4 us
    another operation x1, loops' own time, body(): lax.map(direct_row, jnp.arange(block_side, dtype=jnp.int32))  34 us
    gather x12, local copies, waits for them, and re-layouts, leaf_group(): padded_window[:, rows[:, :, None], columns[:, None, :], :]  32.3 us
    dot_general x4, matrix products, block_group(): jnp.einsum('nijlk,nk->ijl', matrix_imaginary, group_blocks[:, 0], precisi...  15.1 us
    dot_general x4, matrix products, block_group(): jnp.einsum('nijlk,nk->ijl', matrix_real, group_blocks[:, 1], precision=hi...  15.1 us
    dot_general x4, matrix products, block_group(): jnp.einsum('nijlk,nk->ijl', matrix_real, group_blocks[:, 0], precision=hi...  15 us
    dot_general x4, matrix products, block_group(): jnp.einsum('nijlk,nk->ijl', matrix_imaginary, group_blocks[:, 1], precisi...  15 us
  transfers between devices with their start and end apart: 4, of which 1 were waited for; matrix products, arithmetic and copies ran while one was open for 52% of the time, Pallas kernels for 0%

commit v1 on v0

v1 whole, which is shorter than its diff:
```python
import functools
import math

import jax
import jax.numpy as jnp
import numpy as np
from jax import lax
from jax.experimental import pallas as pl
from jax.experimental.pallas import tpu as pltpu
from jax.sharding import PartitionSpec as P

ORDER = 10
DELTA_SQUARED = 0.0025
TWO_PI = 2.0 * math.pi
MESH = pl.DeviceIdType.MESH
CYCLE = [(a, b) for a in range(-2, 3) for b in range(-2, 3) if max(abs(a), abs(b)) == 2]
DIRECTIONS = [(a, b) for a in (-1, 0, 1) for b in (-1, 0, 1) if (a, b) != (0, 0)]
WIDTH = 2
FEATURES = 64
CHUNK = 64
MULTI = 24


def span(step, side):
    return {-1: (0, WIDTH), 0: (0, side), 1: (side - WIDTH, WIDTH)}[step]


def landing(step, side):
    return {1: 0, 0: WIDTH, -1: WIDTH + side}[step]


def moment_columns(base_x, base_y, strength, lane):
    power_x, power_y = strength, jnp.zeros_like(strength)
    out = jnp.zeros(lane.shape, jnp.float32)
    for k in range(ORDER):
        if k:
            power_x, power_y = (
                power_x * base_x - power_y * base_y,
                power_x * base_y + power_y * base_x,
            )
        out = jnp.where(lane == k, jnp.sum(power_x, axis=1, keepdims=True), out)
        if k:
            out = jnp.where(lane == ORDER + k, jnp.sum(power_y, axis=1, keepdims=True), out)
    return out


def exchange_kernel(slabs, leaves, side, *refs):
    part_ref, win_ref, own_ref, near_ref, block_ref = refs[:5]
    sends, recvs = refs[5:13], refs[13:21]
    multi_ref, row_ref = refs[21:23]
    halo_send, halo_recv, multi_send, multi_recv, row_send, row_recv = refs[23:]
    count = slabs * leaves
    window = side + 2 * WIDTH
    slab, leaf = lax.axis_index("slab"), lax.axis_index("leaf")
    me = slab * leaves + leaf

    def place(number):
        return (number // leaves, lax.rem(number, leaves))

    barrier = pltpu.get_barrier_semaphore()

    @pl.loop(1, count)
    def _(o):
        pl.semaphore_signal(
            barrier, inc=1, device_id=place(lax.rem(me + o, count)), device_id_type=MESH
        )

    for c in range(3):
        for i in range(side):
            own_ref[c, i * side : (i + 1) * side, :] = part_ref[c, i]
    win_ref[...] = jnp.zeros_like(win_ref)
    for c in range(3):
        for i in range(side):
            at = (i + WIDTH) * window + WIDTH
            win_ref[c, at : at + side, :] = part_ref[c, i]
    for k, (a, b) in enumerate(DIRECTIONS):
        (i0, ni), (j0, nj) = span(a, side), span(b, side)
        for c in range(3):
            for r in range(ni):
                sends[k][c, r * nj : (r + 1) * nj, :] = part_ref[c, i0 + r, j0 : j0 + nj, :]

    def exists(a, b):
        s, l = slab + a, leaf + b
        return (s >= 0) & (s < slabs) & (l >= 0) & (l < leaves)

    def halo_copy(k):
        a, b = DIRECTIONS[k]
        return pltpu.make_async_remote_copy(
            src_ref=sends[k], dst_ref=recvs[k],
            send_sem=halo_send.at[k], recv_sem=halo_recv.at[k],
            device_id=(slab + a, leaf + b), device_id_type=MESH,
        )

    def multi_copy(k):
        a, b = DIRECTIONS[k]
        return pltpu.make_async_remote_copy(
            src_ref=multi_ref, dst_ref=near_ref.at[(1 - a) * 3 + (1 - b)],
            send_sem=multi_send.at[k], recv_sem=multi_recv.at[k],
            device_id=(slab + a, leaf + b), device_id_type=MESH,
        )

    def row_copy(o):
        return pltpu.make_async_remote_copy(
            src_ref=row_ref, dst_ref=block_ref.at[me],
            send_sem=row_send.at[o], recv_sem=row_recv.at[o],
            device_id=place(lax.rem(me + o, count)), device_id_type=MESH,
        )

    pl.semaphore_wait(barrier, count - 1)
    for k, (a, b) in enumerate(DIRECTIONS):
        @pl.when(exists(a, b))
        def _(k=k):
            halo_copy(k).start()

    own_x, own_y, strength = own_ref[0], own_ref[1], own_ref[2]
    lane = lax.broadcasted_iota(jnp.int32, (side * side, 128), 1)
    number = lax.broadcasted_iota(jnp.int32, own_x.shape, 0)
    centred_x = (number // side).astype(jnp.float32) - (side - 1) / 2.0
    centred_y = (number % side).astype(jnp.float32) - (side - 1) / 2.0
    block = moment_columns(own_x + centred_x, own_y + centred_y, strength, lane)
    row_ref[...] = jnp.sum(block, axis=0, keepdims=True)
    block_ref[me] = row_ref[...]

    @pl.loop(1, count)
    def _(o):
        row_copy(o).start()

    columns = moment_columns(own_x, own_y, strength, lane)
    square = jnp.concatenate(
        [columns, jnp.zeros((128 - side * side, 128), jnp.float32)], axis=0
    )
    multi_ref[...] = square.T[:MULTI]
    near_ref[4] = multi_ref[...]
    for k, (a, b) in enumerate(DIRECTIONS):
        @pl.when(exists(a, b))
        def _(k=k):
            multi_copy(k).start()

        @pl.when(jnp.logical_not(exists(-a, -b)))
        def _(a=a, b=b):
            near_ref[(1 - a) * 3 + (1 - b)] = jnp.zeros((MULTI, 128), jnp.float32)

    for k, (a, b) in enumerate(DIRECTIONS):
        @pl.when(exists(-a, -b))
        def _(k=k, a=a, b=b):
            halo_copy(k).wait_recv()
            (i0, ni), (j0, nj) = span(a, side), span(b, side)
            for c in range(3):
                for r in range(ni):
                    at = (landing(a, side) + r) * window + landing(b, side)
                    win_ref[c, at : at + nj, :] = recvs[k][c, r * nj : (r + 1) * nj, :]
            multi_copy(k).wait_recv()

        @pl.when(exists(a, b))
        def _(k=k):
            halo_copy(k).wait_send()
            multi_copy(k).wait_send()

    @pl.loop(1, count)
    def _(o):
        row_copy(o).wait_recv()
        row_copy(o).wait_send()


def rounded(values):
    return values.astype(jnp.bfloat16).astype(jnp.float32)


def pieces(value, extra):
    coarse = jnp.floor(value * 32.0 + 0.5) * (1.0 / 32.0)
    rest = value - coarse
    rest_1 = rounded(rest)
    rest_2 = rounded(rest - rest_1)
    rest = rest_1 + rest_2
    square = coarse * coarse
    square_1 = rounded(square)
    square_2 = square - square_1
    cross = 2.0 * coarse * rest + (rest * rest + extra)
    cross_1 = rounded(cross)
    cross_2 = rounded(cross - cross_1)
    cross_3 = cross - cross_1 - cross_2
    return dict(
        one=jnp.ones_like(value), h=coarse, l1=rest_1, l2=rest_2, s1=square_1, s2=square_2,
        c1=cross_1, c2=cross_2, c3=cross_3,
    )


STEP_HIGH = [("h", -2.0, "one", 1), ("one", 2.0, "h", 1), ("one", 1.0, "one", 2)]
STEP_LOW = [
    ("l1", -2.0, "one", 1), ("l2", -2.0, "one", 1), ("one", 2.0, "l1", 1), ("one", 2.0, "l2", 1),
]
PLAIN_HIGH = [
    ("s1", 1.0, "one", 0), ("s2", 1.0, "one", 0), ("one", 1.0, "s1", 0), ("one", 1.0, "s2", 0),
    ("h", -2.0, "h", 0),
]
PLAIN_LOW = [
    ("c1", 1.0, "one", 0), ("c2", 1.0, "one", 0), ("c3", 1.0, "one", 0),
    ("one", 1.0, "c1", 0), ("one", 1.0, "c2", 0), ("one", 1.0, "c3", 0),
    ("h", -2.0, "l1", 0), ("h", -2.0, "l2", 0), ("l1", -2.0, "h", 0), ("l2", -2.0, "h", 0),
    ("l1", -2.0, "l1", 0), ("l1", -2.0, "l2", 0), ("l2", -2.0, "l1", 0),
]


def both(rows):
    return [(axis, row) for axis in (0, 1) for row in rows]


HIGH = both(STEP_HIGH) + both(PLAIN_HIGH)
ROWS = HIGH + both(STEP_LOW) + both(PLAIN_LOW)


def step_scales():
    table = np.ones((25, 16, 128), np.float32)
    for number in range(25):
        step = (number // 5 - 2, number % 5 - 2)
        for at, first in ((0, 0), (8, 16)):
            for r in range(8):
                axis, (_, _, _, power) = ROWS[first + r]
                table[number, at + r] = float(step[axis]) ** power
    return table


def field_kernel(
    slabs, leaves, side, mask_ref, win_ref, own_ref, near_ref, block_ref, columns_ref, scale_ref,
    out_ref, source_ref, target_ref, left_ref, right_ref, gain_ref, acc_ref, sum_ref,
):
    count = slabs * leaves
    window = side + 2 * WIDTH
    own = side * side
    particles = own_ref.shape[2]
    halves = particles // 128
    all_leaves = window * window

    def fill(ref, get, leaf_count, side_of):
        for g in range(leaf_count // 8):
            for half in range(halves):
                lanes = slice(half * 128, (half + 1) * 128)
                extra = DELTA_SQUARED / 2.0 if side_of == 0 else 0.0
                parts = [pieces(get(c, g, lanes), extra) for c in range(2)]
                for r in range(FEATURES):
                    if r < len(ROWS):
                        axis, (target, factor, source, _) = ROWS[r]
                        if side_of == 0:
                            value = parts[axis][target] * factor
                        else:
                            value = parts[axis][source]
                    else:
                        value = jnp.zeros((8, 128), jnp.float32)
                    ref[half, r * leaf_count + g * 8 : r * leaf_count + g * 8 + 8, :] = value

    fill(target_ref, lambda c, g, lanes: own_ref[c, g * 8 : g * 8 + 8, lanes], own, 0)
    fill(source_ref, lambda c, g, lanes: win_ref[c, g * 8 : g * 8 + 8, lanes], all_leaves, 1)

    @pl.loop(0, own)
    def _(t):
        ti, tj = t // side, lax.rem(t, side)
        for half in range(halves):
            rows = target_ref[half, pl.ds(t, FEATURES, stride=own), :]
            left_ref[half * 128 : (half + 1) * 128, :] = rows.T.astype(jnp.bfloat16)
        for number in range(25):
            dx, dy = number // 5 - 2, number % 5 - 2
            leaf = (ti + (dx + 2)) * window + tj + (dy + 2)
            for half in range(halves):
                lanes = slice(half * 128, (half + 1) * 128)
                base = source_ref[half, pl.ds(leaf, FEATURES, stride=all_leaves), :]
                scale = scale_ref[number]
                base = jnp.concatenate(
                    [base[:8] * scale[:8], base[8:16], base[16:24] * scale[8:], base[24:]], axis=0
                )
                right_ref[number, :, lanes] = base.astype(jnp.bfloat16)
            strength = win_ref[2, pl.ds(leaf, 1), :]
            if max(abs(dx), abs(dy)) == 2:
                strength = strength * mask_ref[CYCLE.index((dx, dy)), ti, tj].astype(jnp.float32)
            gain_ref[number, 0:1, :] = strength
            gain_ref[number, 1:2, :] = strength * (win_ref[0, pl.ds(leaf, 1), :] + float(dx))
            gain_ref[number, 2:3, :] = strength * (win_ref[1, pl.ds(leaf, 1), :] + float(dy))

        @pl.loop(0, particles // CHUNK)
        def _(chunk):
            at = pl.multiple_of(chunk * CHUNK, CHUNK)
            left = left_ref[pl.ds(at, CHUNK), :]
            totals = [jnp.zeros((CHUNK, 128), jnp.float32) for _ in range(3)]
            for number in range(25):
                distance = jnp.dot(
                    left, right_ref[number], preferred_element_type=jnp.float32
                )
                inverse = pl.reciprocal(distance, approx=True)
                for half in range(halves):
                    lanes = slice(half * 128, (half + 1) * 128)
                    part = inverse[:, lanes]
                    for q in range(3):
                        totals[q] = totals[q] + part * gain_ref[number, q : q + 1, lanes]
            for q in range(3):
                acc_ref[q, pl.ds(at, CHUNK), :] = totals[q]

        for q in range(3):
            sum_ref[q, pl.ds(t, 1), :] = jnp.concatenate(
                [
                    jnp.sum(acc_ref[q, half * 128 : (half + 1) * 128, :].T, axis=0, keepdims=True)
                    for half in range(halves)
                ],
                axis=1,
            )

    slab, leaf = lax.axis_index("slab"), lax.axis_index("leaf")
    in_window = 9 * own
    rows = block_ref[:, 0, :]
    block_lanes = -(-count // 128) * 128
    if block_lanes > count:
        rows = jnp.concatenate(
            [rows, jnp.zeros((block_lanes - count, 128), jnp.float32)], axis=0
        )
    blocks = jnp.concatenate(
        [rows[k * 128 : (k + 1) * 128].T[:MULTI] for k in range(block_lanes // 128)], axis=1
    )
    near_lane = lax.broadcasted_iota(jnp.int32, (MULTI, 128), 1)
    groups = -(-in_window // 128)
    parts = [jnp.zeros((MULTI, 128), jnp.float32) for _ in range(groups)]
    for d in range(9):
        piece = jnp.where(near_lane < own, near_ref[d], 0.0)
        at = d * own
        shift = at % 128
        if shift:
            piece = pltpu.roll(piece, shift, 1)
        parts[at // 128] = parts[at // 128] + piece
    used = in_window % 128
    if used and used + count <= 128:
        first_block = in_window
        parts[-1] = parts[-1] + pltpu.roll(blocks[:, :128], used, 1)
    else:
        first_block = groups * 128
        parts.append(blocks)
    moments = jnp.concatenate(parts, axis=1)
    total_lanes = moments.shape[1]

    lane = lax.broadcasted_iota(jnp.int32, (own, total_lanes), 1)
    row = lax.broadcasted_iota(jnp.int32, (own, total_lanes), 0)
    ti, tj = row // side, row % side
    device = lane // own
    inside = lane % own
    dx = (device // 3 - 1) * side + inside // side - ti
    dy = (device % 3 - 1) * side + inside % side - tj
    reach = jnp.maximum(jnp.abs(dx), jnp.abs(dy))
    weight = jnp.zeros((own, total_lanes), jnp.float32)
    for o, (a, b) in enumerate(CYCLE):
        weight = jnp.where((dx == a) & (dy == b), 1.0 - columns_ref[:, o : o + 1], weight)
    weight = jnp.where(reach >= 3, 1.0, weight)
    weight = jnp.where(lane < in_window, weight, 0.0)
    number = lane - first_block
    block_x, block_y = number // leaves, number % leaves
    remote = (number >= 0) & (number < count) & (
        jnp.maximum(jnp.abs(block_x - slab), jnp.abs(block_y - leaf)) >= 2
    )
    middle = (side - 1) / 2.0
    far_x = ((block_x - slab) * side - ti).astype(jnp.float32) + middle
    far_y = ((block_y - leaf) * side - tj).astype(jnp.float32) + middle
    weight = jnp.where(remote, 1.0, weight)
    shift_x = jnp.where(remote, far_x, dx.astype(jnp.float32))
    shift_y = jnp.where(remote, far_y, dy.astype(jnp.float32))
    shift_x = jnp.where(weight == 0.0, 1.0, shift_x)
    shift_y = jnp.where(weight == 0.0, 0.0, shift_y)
    denominator = shift_x * shift_x + shift_y * shift_y
    base_x, base_y = shift_x / denominator, -shift_y / denominator
    power_x, power_y = [weight * base_x], [weight * base_y]
    for n in range(1, 2 * ORDER - 1):
        last_x, last_y = power_x[-1] * float(n), power_y[-1] * float(n)
        power_x.append(last_x * base_x - last_y * base_y)
        power_y.append(last_x * base_y + last_y * base_x)
    local_x, local_y = [], []
    moment_x = [
        moments[k : k + 1] * ((-1.0) ** (k + 1) / math.factorial(k)) for k in range(ORDER)
    ]
    moment_y = [
        moments[ORDER + k : ORDER + k + 1] * ((-1.0) ** (k + 1) / math.factorial(k))
        for k in range(ORDER)
    ]
    for m in range(ORDER):
        sum_x = jnp.zeros((own, total_lanes), jnp.float32)
        sum_y = jnp.zeros((own, total_lanes), jnp.float32)
        for k in range(ORDER):
            px, py = power_x[m + k], power_y[m + k]
            sum_x = sum_x + (moment_x[k] * px - moment_y[k] * py)
            sum_y = sum_y + (moment_x[k] * py + moment_y[k] * px)
        scale = 1.0 / math.factorial(m)
        local_x.append(jnp.sum(sum_x, axis=1, keepdims=True) * scale)
        local_y.append(jnp.sum(sum_y, axis=1, keepdims=True) * scale)

    own_x, own_y = own_ref[0], own_ref[1]
    field_x = jnp.broadcast_to(local_x[-1], own_x.shape)
    field_y = jnp.broadcast_to(local_y[-1], own_x.shape)
    for m in range(ORDER - 2, -1, -1):
        field_x, field_y = (
            field_x * own_x - field_y * own_y + local_x[m],
            field_x * own_y + field_y * own_x + local_y[m],
        )
    first = (sum_ref[2] - own_y * sum_ref[0] + field_y) * (1.0 / TWO_PI)
    second = (own_x * sum_ref[0] - sum_ref[1] + field_x) * (1.0 / TWO_PI)
    for i in range(side):
        out_ref[0, i] = first[i * side : (i + 1) * side]
        out_ref[1, i] = second[i * side : (i + 1) * side]


def body(particles, near_mask, *, slabs, leaves):
    side, count = particles.shape[1], particles.shape[3]
    own = side * side
    window = side + 2 * WIDTH
    devices = slabs * leaves
    f32 = jnp.float32
    vmem = pl.BlockSpec(memory_space=pltpu.VMEM)
    smem = pl.BlockSpec(memory_space=pltpu.SMEM)
    strips = [
        pltpu.VMEM((3, span(a, side)[1] * span(b, side)[1], count), f32) for a, b in DIRECTIONS
    ]
    win, own_part, near, blocks = pl.pallas_call(
        functools.partial(exchange_kernel, slabs, leaves, side),
        out_shape=(
            jax.ShapeDtypeStruct((3, window * window, count), f32),
            jax.ShapeDtypeStruct((3, own, count), f32),
            jax.ShapeDtypeStruct((9, MULTI, 128), f32),
            jax.ShapeDtypeStruct((devices, 1, 128), f32),
        ),
        in_specs=[vmem],
        out_specs=(vmem, vmem, vmem, vmem),
        scratch_shapes=strips + strips + [
            pltpu.VMEM((MULTI, 128), f32),
            pltpu.VMEM((1, 128), f32),
            pltpu.SemaphoreType.DMA((8,)), pltpu.SemaphoreType.DMA((8,)),
            pltpu.SemaphoreType.DMA((8,)), pltpu.SemaphoreType.DMA((8,)),
            pltpu.SemaphoreType.DMA((devices,)), pltpu.SemaphoreType.DMA((devices,)),
        ],
        compiler_params=pltpu.CompilerParams(collective_id=0, has_side_effects=True),
        name="exchange",
    )(particles)
    columns = near_mask.reshape(len(CYCLE), own).T.astype(f32)
    bf16 = jnp.bfloat16
    return pl.pallas_call(
        functools.partial(field_kernel, slabs, leaves, side),
        out_shape=jax.ShapeDtypeStruct((2, side, side, count), f32),
        in_specs=[smem] + [vmem] * 6,
        out_specs=vmem,
        scratch_shapes=[
            pltpu.VMEM((count // 128, FEATURES * window * window, 128), f32),
            pltpu.VMEM((count // 128, FEATURES * own, 128), f32),
            pltpu.VMEM((count, FEATURES), bf16),
            pltpu.VMEM((25, FEATURES, count), bf16),
            pltpu.VMEM((25, 8, count), f32),
            pltpu.VMEM((3, count, 128), f32),
            pltpu.VMEM((3, own, count), f32),
        ],
        compiler_params=pltpu.CompilerParams(vmem_limit_bytes=48 * 1024 * 1024),
        name="field",
    )(near_mask, win, own_part, near, blocks, columns, jnp.asarray(step_scales()))


def solution(mesh):
    return jax.shard_map(
        functools.partial(body, slabs=mesh.shape["slab"], leaves=mesh.shape["leaf"]),
        mesh=mesh,
        in_specs=(P(None, "slab", "leaf", None), P(None, "slab", "leaf")),
        out_specs=P(None, "slab", "leaf", None),
        check_vma=False,
    )
```

time: 324 us -> 89.8 us (0.28)
  Pallas kernels: 0 us -> 84.2 us
  other arithmetic: 78.6 us -> 0.77 us
  local copies, waits for them, and re-layouts: 80.3 us -> 4.37 us
  matrix products: 70.1 us -> 0 us
  blocking collectives: 44.4 us -> 0 us
  loops' own time: 35.3 us -> 0 us
  starting transfers between devices: 9.67 us -> 0 us
    pallas_call x0 -> x2, Pallas kernels: none -> 84.2 us  [the longest x1 70.9 us: body(): pl.pallas_call(functools.partial(field_kernel, slabs, leaves, side), out_...]
    dot_general x44 -> x0, matrix products: 70.1 us -> none  [the longest x4 15.1 us: block_group(): jnp.einsum('nijlk,nk->ijl', matrix_imaginary, group_blocks[:, 0], precisi...]
    gather x56 -> x0, local copies, waits for them, and re-layouts: 60.3 us -> none  [the longest x12 32.3 us: leaf_group(): padded_window[:, rows[:, :, None], columns[:, None, :], :]]
    reduce_sum x22 -> x0, other arithmetic: 56.3 us -> none  [the longest x20 55.9 us: direct_row(): row_imaginary = row_imaginary - jnp.sum(factor * delta_y, -1)]
    all_gather x1 -> x0, blocking collectives: 44.4 us -> none  [body(): lax.all_gather(leaf_multipole[None], ('slab', 'leaf'), axis=0, tiled=True)]
    another operation x3 -> x0, loops' own time: 35.3 us -> none  [the longest x1 34 us: body(): lax.map(direct_row, jnp.arange(block_side, dtype=jnp.int32))]
    ppermute x4 -> x0, starting transfers between devices: 9.67 us -> none  [the longest x2 7.09 us: with_halo(): before = lax.ppermute(last, axis, up)]
    while x136 -> x0, other arithmetic: 7.95 us -> none
  transfers between devices with their start and end apart: 4 -> 0, of which waited for: 1 -> 0; matrix products, arithmetic and copies ran while one was open for 52% -> 0% of each run, Pallas kernels for 0% -> 0%
where the time goes in v1:
time: 89.8 us; the launch traced here: 89.4 us
  Pallas kernels  84.2 us (94%)
  local copies, waits for them, and re-layouts  4.37 us (5%)
    pallas_call x1, Pallas kernels, body(): pl.pallas_call(functools.partial(field_kernel, slabs, leaves, side), out_...  70.9 us
    pallas_call x1, Pallas kernels, body(): pl.pallas_call(functools.partial(exchange_kernel, slabs, leaves, side), o...  13.3 us
    unnamed x13, local copies, waits for them, and re-layouts  4.37 us

profile of v1, /device:TPU:0, one launch (start us, length us, event | category | flops | bytes accessed | tf_op | source)
XLA Modules:
  0.0 89.4 jit_solution(2796422078352081975)
XLA Ops:
  0.0 0.0 copy-start.5
  0.0 0.8 convert_element_type.7
  0.8 0.0 copy-done.5
  0.8 0.1 copy.4.mask_ref
  0.9 13.3 %exchange.1 = (f32[3,64,256]{2,1,0:T(8,128)}, f32[3,16,256]{2,1,0:T(8,128)}, f32[9,24,128]{2,1,0:T(8,128)}, f32[32,1,128]{2,1,0:T(1,128)}) custom-call(f32[3,4,4,256]{3,2,1,0:T(4,128)} %refs_0_.1), custom_call_target="tpu_custom_call" | custom-call | tf_op jit(solution)/shard_map/exchange/pallas_call | solution.py:414
  14.2 0.0 copy-start
  14.2 0.9 %copy-done = f32[25,16,128]{2,1,0:T(8,128)S(1)} copy-done((f32[25,16,128]{2,1,0:T(8,128)S(1)}, f32[25,16,128]{2,1,0:T(8,128)}, u32[]{:S(2)}) %copy-start) | copy-done | bytes 204824
  15.1 0.0 copy-start.1
  15.1 0.9 %copy-done.1 = f32[3,64,256]{2,1,0:T(8,128)S(1)} copy-done((f32[3,64,256]{2,1,0:T(8,128)S(1)}, f32[3,64,256]{2,1,0:T(8,128)}, u32[]{:S(2)}) %copy-start.1) | copy-done | bytes 196632
  16.1 0.0 copy-start.2
  16.1 0.9 %copy-done.2 = f32[9,24,128]{2,1,0:T(8,128)S(1)} copy-done((f32[9,24,128]{2,1,0:T(8,128)S(1)}, f32[9,24,128]{2,1,0:T(8,128)}, u32[]{:S(2)}) %copy-start.2) | copy-done | bytes 110616
  17.0 0.0 copy-start.3
  17.0 0.8 copy-done.3
  17.8 0.0 copy-start.4
  17.8 0.7 copy-done.4
  18.5 70.9 %field.1 = f32[2,4,4,256]{3,2,1,0:T(4,128)} custom-call(s32[16,4,4]{2,1,0:T(4,128)S(1)} %copy.4.mask_ref, f32[3,64,256]{2,1,0:T(8,128)S(1)} %copy-done.1, f32[3,16,256]{2,1,0:T(8,128)S(1)} %copy-done.3, f32[9,24,128]{2,1,0:T(8,128)S(1)} %copy-done.2, f32[32,1,128]{2,1,0:T(1,128)S(1)} %copy-done.4, f32[16,16]{1,0:T(8,128)S(1)} %bitcast.3, ...), custom_call_target="tpu_custom_call" | custom-call | tf_op jit(solution)/shard_map/field/pallas_call | solution.py:436
Async XLA Ops:
  0.0 0.8 copy-start.5
  14.2 0.9 %copy-start = (f32[25,16,128]{2,1,0:T(8,128)S(1)}, f32[25,16,128]{2,1,0:T(8,128)}, u32[]{:S(2)}) copy-start(f32[25,16,128]{2,1,0:T(8,128)} %constant.2.clone.scale_ref) | copy-start | bytes 614404
  15.1 0.9 %copy-start.1 = (f32[3,64,256]{2,1,0:T(8,128)S(1)}, f32[3,64,256]{2,1,0:T(8,128)}, u32[]{:S(2)}) copy-start(f32[3,64,256]{2,1,0:T(8,128)} %get-tuple-element.9.win_ref) | copy-start | bytes 589828
  16.1 0.9 %copy-start.2 = (f32[9,24,128]{2,1,0:T(8,128)S(1)}, f32[9,24,128]{2,1,0:T(8,128)}, u32[]{:S(2)}) copy-start(f32[9,24,128]{2,1,0:T(8,128)} %get-tuple-element.11.near_ref) | copy-start | bytes 331780
  17.0 0.8 copy-start.3
  17.8 0.7 copy-start.4

commit v2 on v1

--- a/solution.py
+++ b/solution.py
@@ -16,7 +16,7 @@
 CYCLE = [(a, b) for a in range(-2, 3) for b in range(-2, 3) if max(abs(a), abs(b)) == 2]
 DIRECTIONS = [(a, b) for a in (-1, 0, 1) for b in (-1, 0, 1) if (a, b) != (0, 0)]
 WIDTH = 2
-FEATURES = 64
+FEATURES = 48
 CHUNK = 64
 MULTI = 24
 
@@ -166,12 +166,13 @@
     return values.astype(jnp.bfloat16).astype(jnp.float32)
 
 
-def pieces(value, extra):
+def pieces(value, place, extra):
     coarse = jnp.floor(value * 32.0 + 0.5) * (1.0 / 32.0)
     rest = value - coarse
     rest_1 = rounded(rest)
     rest_2 = rounded(rest - rest_1)
     rest = rest_1 + rest_2
+    coarse = coarse + place
     square = coarse * coarse
     square_1 = rounded(square)
     square_2 = square - square_1
@@ -185,43 +186,21 @@
     )
 
 
-STEP_HIGH = [("h", -2.0, "one", 1), ("one", 2.0, "h", 1), ("one", 1.0, "one", 2)]
-STEP_LOW = [
-    ("l1", -2.0, "one", 1), ("l2", -2.0, "one", 1), ("one", 2.0, "l1", 1), ("one", 2.0, "l2", 1),
+HIGH = [
+    ("s1", 1.0, "one"), ("s2", 1.0, "one"), ("one", 1.0, "s1"), ("one", 1.0, "s2"),
+    ("h", -2.0, "h"),
 ]
-PLAIN_HIGH = [
-    ("s1", 1.0, "one", 0), ("s2", 1.0, "one", 0), ("one", 1.0, "s1", 0), ("one", 1.0, "s2", 0),
-    ("h", -2.0, "h", 0),
+LOW = [
+    ("c1", 1.0, "one"), ("c2", 1.0, "one"), ("c3", 1.0, "one"),
+    ("one", 1.0, "c1"), ("one", 1.0, "c2"), ("one", 1.0, "c3"),
+    ("h", -2.0, "l1"), ("h", -2.0, "l2"), ("l1", -2.0, "h"), ("l2", -2.0, "h"),
+    ("l1", -2.0, "l1"), ("l1", -2.0, "l2"), ("l2", -2.0, "l1"),
 ]
-PLAIN_LOW = [
-    ("c1", 1.0, "one", 0), ("c2", 1.0, "one", 0), ("c3", 1.0, "one", 0),
-    ("one", 1.0, "c1", 0), ("one", 1.0, "c2", 0), ("one", 1.0, "c3", 0),
-    ("h", -2.0, "l1", 0), ("h", -2.0, "l2", 0), ("l1", -2.0, "h", 0), ("l2", -2.0, "h", 0),
-    ("l1", -2.0, "l1", 0), ("l1", -2.0, "l2", 0), ("l2", -2.0, "l1", 0),
-]
-
-
-def both(rows):
-    return [(axis, row) for axis in (0, 1) for row in rows]
-
-
-HIGH = both(STEP_HIGH) + both(PLAIN_HIGH)
-ROWS = HIGH + both(STEP_LOW) + both(PLAIN_LOW)
-
-
-def step_scales():
-    table = np.ones((25, 16, 128), np.float32)
-    for number in range(25):
-        step = (number // 5 - 2, number % 5 - 2)
-        for at, first in ((0, 0), (8, 16)):
-            for r in range(8):
-                axis, (_, _, _, power) = ROWS[first + r]
-                table[number, at + r] = float(step[axis]) ** power
-    return table
+ROWS = [(axis, row) for rows in (HIGH, LOW) for axis in (0, 1) for row in rows]
 
 
 def field_kernel(
-    slabs, leaves, side, mask_ref, win_ref, own_ref, near_ref, block_ref, columns_ref, scale_ref,
+    slabs, leaves, side, mask_ref, win_ref, own_ref, near_ref, block_ref, columns_ref,
     out_ref, source_ref, target_ref, left_ref, right_ref, gain_ref, acc_ref, sum_ref,
 ):
     count = slabs * leaves
@@ -231,43 +210,48 @@
     halves = particles // 128
     all_leaves = window * window
 
-    def fill(ref, get, leaf_count, side_of):
+    def fill(ref, get, width, is_target):
+        leaf_count = width * width
+        stride = leaf_count + 8
+        index = lax.broadcasted_iota(jnp.int32, (8, 128), 0)
+        low = 0 if is_target else WIDTH
         for g in range(leaf_count // 8):
+            place_x = ((index + g * 8) // width - low).astype(jnp.float32) - (side - 1) / 2.0
+            place_y = ((index + g * 8) % width - low).astype(jnp.float32) - (side - 1) / 2.0
             for half in range(halves):
                 lanes = slice(half * 128, (half + 1) * 128)
-                extra = DELTA_SQUARED / 2.0 if side_of == 0 else 0.0
-                parts = [pieces(get(c, g, lanes), extra) for c in range(2)]
+                extra = DELTA_SQUARED / 2.0 if is_target else 0.0
+                parts = [
+                    pieces(get(c, g, lanes), place, extra)
+                    for c, place in ((0, place_x), (1, place_y))
+                ]
                 for r in range(FEATURES):
                     if r < len(ROWS):
-                        axis, (target, factor, source, _) = ROWS[r]
-                        if side_of == 0:
-                            value = parts[axis][target] * factor
-                        else:
-                            value = parts[axis][source]
+                        axis, (target, factor, source) = ROWS[r]
+                        value = parts[axis][target] * factor if is_target else parts[axis][source]
                     else:
                         value = jnp.zeros((8, 128), jnp.float32)
-                    ref[half, r * leaf_count + g * 8 : r * leaf_count + g * 8 + 8, :] = value
-
-    fill(target_ref, lambda c, g, lanes: own_ref[c, g * 8 : g * 8 + 8, lanes], own, 0)
-    fill(source_ref, lambda c, g, lanes: win_ref[c, g * 8 : g * 8 + 8, lanes], all_leaves, 1)
+                    ref[half, r * stride + g * 8 : r * stride + g * 8 + 8, :] = value
+
+    fill(target_ref, lambda c, g, lanes: own_ref[c, g * 8 : g * 8 + 8, lanes], side, True)
+    fill(source_ref, lambda c, g, lanes: win_ref[c, g * 8 : g * 8 + 8, lanes], window, False)
+
+    @pl.loop(0, all_leaves)
+    def _(leaf):
+        for half in range(halves):
+            lanes = slice(half * 128, (half + 1) * 128)
+            rows = source_ref[half, pl.ds(leaf, FEATURES, stride=all_leaves + 8), :]
+            right_ref[leaf, :, lanes] = rows.astype(jnp.bfloat16)
 
     @pl.loop(0, own)
     def _(t):
         ti, tj = t // side, lax.rem(t, side)
         for half in range(halves):
-            rows = target_ref[half, pl.ds(t, FEATURES, stride=own), :]
+            rows = target_ref[half, pl.ds(t, FEATURES, stride=own + 8), :]
             left_ref[half * 128 : (half + 1) * 128, :] = rows.T.astype(jnp.bfloat16)
         for number in range(25):
             dx, dy = number // 5 - 2, number % 5 - 2
             leaf = (ti + (dx + 2)) * window + tj + (dy + 2)
-            for half in range(halves):
-                lanes = slice(half * 128, (half + 1) * 128)
-                base = source_ref[half, pl.ds(leaf, FEATURES, stride=all_leaves), :]
-                scale = scale_ref[number]
-                base = jnp.concatenate(
-                    [base[:8] * scale[:8], base[8:16], base[16:24] * scale[8:], base[24:]], axis=0
-                )
-                right_ref[number, :, lanes] = base.astype(jnp.bfloat16)
             strength = win_ref[2, pl.ds(leaf, 1), :]
             if max(abs(dx), abs(dy)) == 2:
                 strength = strength * mask_ref[CYCLE.index((dx, dy)), ti, tj].astype(jnp.float32)
@@ -281,9 +265,8 @@
             left = left_ref[pl.ds(at, CHUNK), :]
             totals = [jnp.zeros((CHUNK, 128), jnp.float32) for _ in range(3)]
             for number in range(25):
-                distance = jnp.dot(
-                    left, right_ref[number], preferred_element_type=jnp.float32
-                )
+                leaf = (ti + number // 5) * window + tj + number % 5
+                distance = jnp.dot(left, right_ref[leaf], preferred_element_type=jnp.float32)
                 inverse = pl.reciprocal(distance, approx=True)
                 for half in range(halves):
                     lanes = slice(half * 128, (half + 1) * 128)
@@ -436,20 +419,20 @@
     return pl.pallas_call(
         functools.partial(field_kernel, slabs, leaves, side),
         out_shape=jax.ShapeDtypeStruct((2, side, side, count), f32),
-        in_specs=[smem] + [vmem] * 6,
+        in_specs=[smem] + [vmem] * 5,
         out_specs=vmem,
         scratch_shapes=[
-            pltpu.VMEM((count // 128, FEATURES * window * window, 128), f32),
-            pltpu.VMEM((count // 128, FEATURES * own, 128), f32),
+            pltpu.VMEM((count // 128, FEATURES * (window * window + 8), 128), f32),
+            pltpu.VMEM((count // 128, FEATURES * (own + 8), 128), f32),
             pltpu.VMEM((count, FEATURES), bf16),
-            pltpu.VMEM((25, FEATURES, count), bf16),
+            pltpu.VMEM((window * window, FEATURES, count), bf16),
             pltpu.VMEM((25, 8, count), f32),
             pltpu.VMEM((3, count, 128), f32),
             pltpu.VMEM((3, own, count), f32),
         ],
         compiler_params=pltpu.CompilerParams(vmem_limit_bytes=48 * 1024 * 1024),
         name="field",
-    )(near_mask, win, own_part, near, blocks, columns, jnp.asarray(step_scales()))
+    )(near_mask, win, own_part, near, blocks, columns)
 
 
 def solution(mesh):

time: 89.8 us -> 67.2 us (0.75)
  Pallas kernels: 84.2 us -> 62.6 us
  local copies, waits for them, and re-layouts: 4.37 us -> 3.44 us
    pallas_call x1, Pallas kernels: 70.9 us -> 49.3 us  [body(): pl.pallas_call(functools.partial(field_kernel, slabs, leaves, side), out_...]
    unnamed x13 -> x11, local copies, waits for them, and re-layouts: 4.37 us -> 3.44 us
where the time goes in v2:
time: 67.2 us; the launch traced here: 66.9 us
  Pallas kernels  62.6 us (93%)
  local copies, waits for them, and re-layouts  3.44 us (5%)
  other arithmetic  0.77 us (1%)
    pallas_call x1, Pallas kernels, body(): pl.pallas_call(functools.partial(field_kernel, slabs, leaves, side), out_...  49.3 us
    pallas_call x1, Pallas kernels, body(): pl.pallas_call(functools.partial(exchange_kernel, slabs, leaves, side), o...  13.3 us
    unnamed x11, local copies, waits for them, and re-layouts  3.44 us

profile of v2, /device:TPU:0, one launch (start us, length us, event | category | flops | bytes accessed | tf_op | source)
XLA Modules:
  0.0 66.9 jit_solution(3373863140557853492)
XLA Ops:
  0.0 0.0 copy-start.4
  0.0 0.8 %convert_element_type.7 = f32[16,4,4]{0,2,1:T(4,128)S(1)} convert(s32[16,4,4]{0,2,1:T(4,128)} %param.3) | non-fusion elementwise | flops 256 | bytes 2048 | tf_op jit(solution)/shard_map/convert_element_type | solution.py:417
  0.8 0.0 copy-done.4
  0.8 0.1 copy.3.mask_ref
  0.9 13.3 %exchange.1 = (f32[3,64,256]{2,1,0:T(8,128)}, f32[3,16,256]{2,1,0:T(8,128)}, f32[9,24,128]{2,1,0:T(8,128)}, f32[32,1,128]{2,1,0:T(1,128)}) custom-call(f32[3,4,4,256]{3,2,1,0:T(4,128)} %refs_0_.1), custom_call_target="tpu_custom_call" | custom-call | tf_op jit(solution)/shard_map/exchange/pallas_call | solution.py:397
  14.2 0.0 copy-start
  14.2 0.9 %copy-done = f32[3,64,256]{2,1,0:T(8,128)S(1)} copy-done((f32[3,64,256]{2,1,0:T(8,128)S(1)}, f32[3,64,256]{2,1,0:T(8,128)}, u32[]{:S(2)}) %copy-start) | copy-done | bytes 196632
  15.1 0.0 copy-start.1
  15.1 0.9 %copy-done.1 = f32[9,24,128]{2,1,0:T(8,128)S(1)} copy-done((f32[9,24,128]{2,1,0:T(8,128)S(1)}, f32[9,24,128]{2,1,0:T(8,128)}, u32[]{:S(2)}) %copy-start.1) | copy-done | bytes 110616
  16.0 0.0 copy-start.2
  16.0 0.8 %copy-done.2 = f32[3,16,256]{2,1,0:T(8,128)S(1)} copy-done((f32[3,16,256]{2,1,0:T(8,128)S(1)}, f32[3,16,256]{2,1,0:T(8,128)}, u32[]{:S(2)}) %copy-start.2) | copy-done | bytes 49176
  16.8 0.0 copy-start.3
  16.8 0.7 %copy-done.3 = f32[32,1,128]{2,1,0:T(1,128)S(1)} copy-done((f32[32,1,128]{2,1,0:T(1,128)S(1)}, f32[32,1,128]{2,1,0:T(1,128)}, u32[]{:S(2)}) %copy-start.3) | copy-done | bytes 16408
  17.5 49.3 %field.1 = f32[2,4,4,256]{3,2,1,0:T(4,128)} custom-call(s32[16,4,4]{2,1,0:T(4,128)S(1)} %copy.3.mask_ref, f32[3,64,256]{2,1,0:T(8,128)S(1)} %copy-done, f32[3,16,256]{2,1,0:T(8,128)S(1)} %copy-done.2, f32[9,24,128]{2,1,0:T(8,128)S(1)} %copy-done.1, f32[32,1,128]{2,1,0:T(1,128)S(1)} %copy-done.3, f32[16,16]{1,0:T(8,128)S(1)} %bitcast.3), custom_call_target="tpu_custom_call" | custom-call | tf_op jit(solution)/shard_map/field/pallas_call | solution.py:419
Async XLA Ops:
  0.0 0.8 %copy-start.4 = (s32[16,4,4]{0,2,1:T(4,128)S(1)}, s32[16,4,4]{0,2,1:T(4,128)}, u32[]{:S(2)}) copy-start(s32[16,4,4]{0,2,1:T(4,128)} %param.3) | copy-start | bytes 3076
  14.2 0.9 %copy-start = (f32[3,64,256]{2,1,0:T(8,128)S(1)}, f32[3,64,256]{2,1,0:T(8,128)}, u32[]{:S(2)}) copy-start(f32[3,64,256]{2,1,0:T(8,128)} %get-tuple-element.9.win_ref) | copy-start | bytes 589828
  15.1 0.9 %copy-start.1 = (f32[9,24,128]{2,1,0:T(8,128)S(1)}, f32[9,24,128]{2,1,0:T(8,128)}, u32[]{:S(2)}) copy-start(f32[9,24,128]{2,1,0:T(8,128)} %get-tuple-element.11.near_ref) | copy-start | bytes 331780
  16.0 0.8 %copy-start.2 = (f32[3,16,256]{2,1,0:T(8,128)S(1)}, f32[3,16,256]{2,1,0:T(8,128)}, u32[]{:S(2)}) copy-start(f32[3,16,256]{2,1,0:T(8,128)} %get-tuple-element.10.own_ref) | copy-start | bytes 147460
  16.8 0.7 %copy-start.3 = (f32[32,1,128]{2,1,0:T(1,128)S(1)}, f32[32,1,128]{2,1,0:T(1,128)}, u32[]{:S(2)}) copy-start(f32[32,1,128]{2,1,0:T(1,128)} %get-tuple-element.12.block_ref) | copy-start | bytes 49156
